TPU v7x, 512 devices: a whole 4x4x16 slice. The times are simulated.
512 devices in a mesh: lag: 16 (over y, x_hi, core), row: 32 (over z, x_lo).
Axes of the slice: x: 4 (x_hi: 2, x_lo: 2; x = x_hi * 2 + x_lo), y: 4, z: 16, core: 2. Of those that a mesh axis runs over, the one named last changes fastest.
Arguments:
- lag_ops: float32 [32, 3072, 3072], P('lag', 'row'), may hold values from -0.109375 to 0.109375
- inverse: float32 [3072, 3072], P('row'), may hold values from -0.109375 to 0.109375
- history: float32 [32, 3072, 128], P('lag', 'row'), may hold values from -6 to 6
- loads: float32 [3, 3072, 128], P(None, 'row'), may hold values from -6 to 6
Outputs:
- current: float32 [3072, 128], P('row')
- future: float32 [32, 3072, 128], P('lag', 'row')
All inputs are finite; a program needn't handle non-finite values.
Results may differ from a plain program's by a relative error of at most 0.00011.
Values sent between devices are 32-bit elements; how exact they have to be, the bound alone decides.
A program may use at most 64 MiB of HBM per device.

v0:
```python
import jax
import jax.numpy as jnp
from jax import lax
from jax.sharding import PartitionSpec as P

STEPS = 3


def broadcast(array, axis, root):
    mine = lax.axis_index(axis) == root
    return lax.psum(jnp.where(mine, array, jnp.zeros_like(array)), axis)


def from_behind(array, axis, by):
    length = lax.axis_size(axis)
    pairs = [(i, i + by) for i in range(length) if 0 <= i + by < length]
    return lax.ppermute(array, axis, pairs)


def body(lag_ops, inverse, history, loads):
    acc = history
    local_lags = lag_ops.shape[0]
    local_rows = lag_ops.shape[1]
    total_cols = lag_ops.shape[2]
    loads_width = history.shape[2]
    flat_ops = lag_ops.reshape(local_lags * local_rows, total_cols)
    current = jnp.zeros((local_rows, loads_width), jnp.float32)
    for step in range(STEPS):
        rhs = broadcast(loads[step] - acc[0], "lag", 0)
        current = jnp.dot(
            inverse,
            lax.all_gather(rhs, "row", axis=0, tiled=True),
            precision=lax.Precision.HIGHEST,
            preferred_element_type=jnp.float32,
        )
        product = jnp.dot(
            flat_ops,
            lax.all_gather(current, "row", axis=0, tiled=True),
            precision=lax.Precision.HIGHEST,
            preferred_element_type=jnp.float32,
        )
        product = product.reshape(local_lags, local_rows, loads_width)
        incoming = from_behind(acc[0], "lag", -1)
        shifted = jnp.concatenate([acc[1:], incoming[None]], axis=0)
        acc = shifted + product
    return (current, acc)


def solution(mesh):
    placed = (P("lag", "row", None), P("row", None), P("lag", "row", None), P(None, "row", None))
    return jax.shard_map(
        body,
        mesh=mesh,
        in_specs=placed,
        out_specs=(P("row", None), P("lag", "row", None)),
        check_vma=False,
    )
```

profile of v0, /device:TPU:16, one launch (start us, length us, event | category | flops | bytes accessed | tf_op | source)
XLA Modules:
  0.0 1025.2 jit_solution(1420821375179951040)
XLA Ops:
  7.2 1.0 fusion.1
  8.2 58.1 %psum.21 = f32[96,128]{1,0:T(8,128)} all-reduce(f32[96,128]{1,0:T(8,128)S(1)} %fusion.1), channel_id=1, replica_groups=mesh['lag'=16,'row'=32] {'lag'}, use_global_device_ids=true, to_apply=%region_0.1 | all-reduce | flops 12288 | bytes 98304 | tf_op jit(solution)/shard_map/psum | solution.py:11
  66.4 144.5 %all-gather.7.cloned.1.call-done = f32[3072,128]{1,0:T(8,128)} async-done(((f32[96,128]{1,0:T(8,128)}), f32[3072,128]{1,0:T(8,128)}) %all-gather.7.cloned.1.call-update) | async-done | bytes 1572880 | tf_op jit(solution)/shard_map/all_gather | solution.py:32
  210.9 3.8 convolution_bitcast_fusion.2
  215.4 1.9 collective-permute-start
  217.3 128.8 %all-gather.9.cloned.1.call-done = f32[3072,128]{1,0:T(8,128)} async-done(((f32[96,128]{1,0:T(8,128)}), f32[3072,128]{1,0:T(8,128)}) %all-gather.9.cloned.1.call-update) | async-done | bytes 1572880 | tf_op jit(solution)/shard_map/all_gather | solution.py:38
  346.1 3.5 fusion.6
  349.6 0.8 maximum_add_fusion
  351.1 1.4 fusion
  352.5 56.5 %psum.22 = f32[96,128]{1,0:T(8,128)} all-reduce(f32[96,128]{1,0:T(8,128)} %fusion), channel_id=1, replica_groups=mesh['lag'=16,'row'=32] {'lag'}, use_global_device_ids=true, to_apply=%region_1.2 | all-reduce | flops 12288 | bytes 98304 | tf_op jit(solution)/shard_map/psum | solution.py:11
  409.0 136.3 %all-gather.11.cloned.1.call-done = f32[3072,128]{1,0:T(8,128)} async-done(((f32[96,128]{1,0:T(8,128)}), f32[3072,128]{1,0:T(8,128)}) %all-gather.11.cloned.1.call-update) | async-done | bytes 1572880 | tf_op jit(solution)/shard_map/all_gather | solution.py:32
  545.4 3.5 convolution_bitcast_fusion.1
  548.9 1.5 fusion.4
  550.4 1.9 collective-permute-start.1
  552.3 127.9 %all-gather.13.cloned.1.call-done = f32[3072,128]{1,0:T(8,128)} async-done(((f32[96,128]{1,0:T(8,128)}), f32[3072,128]{1,0:T(8,128)}) %all-gather.13.cloned.1.call-update) | async-done | bytes 1572880 | tf_op jit(solution)/shard_map/all_gather | solution.py:38
  680.2 3.4 fusion.7
  685.1 1.4 fusion.2
  686.5 56.5 %psum.23 = f32[96,128]{1,0:T(8,128)} all-reduce(f32[96,128]{1,0:T(8,128)} %fusion.2), channel_id=1, replica_groups=mesh['lag'=16,'row'=32] {'lag'}, use_global_device_ids=true, to_apply=%region_2.3 | all-reduce | flops 12288 | bytes 98304 | tf_op jit(solution)/shard_map/psum | solution.py:11
  743.1 136.4 %all-gather.15.cloned.1.call-done = f32[3072,128]{1,0:T(8,128)} async-done(((f32[96,128]{1,0:T(8,128)}), f32[3072,128]{1,0:T(8,128)}) %all-gather.15.cloned.1.call-update) | async-done | bytes 1572880 | tf_op jit(solution)/shard_map/all_gather | solution.py:32
  879.4 3.5 convolution_bitcast_fusion
  882.9 0.8 fusion.3
  883.8 1.9 collective-permute-start.2
  885.7 128.6 %all-gather.17.cloned.1.call-done = f32[3072,128]{1,0:T(8,128)} async-done(((f32[96,128]{1,0:T(8,128)}), f32[3072,128]{1,0:T(8,128)}) %all-gather.17.cloned.1.call-update) | async-done | bytes 1572880 | tf_op jit(solution)/shard_map/all_gather | solution.py:38
  1014.3 3.4 fusion.8
  (32 shorter events, 3.7 us)
Async XLA Ops:
  7.2 338.9 %copy-start = (f32[2,96,3072]{2,1,0:T(8,128)S(1)}, f32[2,96,3072]{2,1,0:T(8,128)}, u32[]{:S(2)}) copy-start(f32[2,96,3072]{2,1,0:T(8,128)} %param.4) | copy-start | bytes 7077892
  7.2 203.7 %all-gather.7.cloned.1.call-start = ((), (), s32[]{:S(2)}) async-start(), calls=%async_computation | async-start | bytes 1622016 | tf_op jit(solution)/shard_map/all_gather | solution.py:32
  7.2 207.5 %copy-start.4 = (f32[2,96,128]{2,1,0:T(8,128)S(1)}, f32[2,96,128]{2,1,0:T(8,128)}, u32[]{:S(2)}) copy-start(f32[2,96,128]{2,1,0:T(8,128)} %param.6) | copy-start | bytes 294916
  66.4 279.7 %all-gather.9.cloned.1.call-start = ((), (), s32[]{:S(2)}) async-start(), calls=%async_computation.1 | async-start | bytes 1622016 | tf_op jit(solution)/shard_map/all_gather | solution.py:38
  214.7 330.7 %all-gather.11.cloned.1.call-start = ((), (), s32[]{:S(2)}) async-start(), calls=%async_computation.2 | async-start | bytes 1622016 | tf_op jit(solution)/shard_map/all_gather | solution.py:32
  215.4 134.2 %collective-permute-start = (f32[96,128]{1,0:T(8,128)}, f32[96,128]{1,0:T(8,128)}, u32[]{:S(2)}, u32[]{:S(2)}) collective-permute-start(f32[96,128]{1,0:T(8,128)} %get-tuple-element.7), channel_id=1, source_target_pairs={{32,0},{64,32},{96,64},{128,96},{160,128},{192,160},{224,192},{256... | collective-permute-start | bytes 147464 | tf_op jit(solution)/shard_map/ppermute | solution.py:17
  346.1 3.5 copy-start.6
  346.1 199.3 %copy-start.1 = (f32[96,3072]{1,0:T(8,128)S(1)}, f32[96,3072]{1,0:T(8,128)}, u32[]{:S(2)}) copy-start(f32[96,3072]{1,0:T(8,128)} %param.5) | copy-start | bytes 3538948
  350.4 0.6 copy-start.2
  409.0 271.2 %all-gather.13.cloned.1.call-start = ((), (), s32[]{:S(2)}) async-start(), calls=%async_computation.3 | async-start | bytes 1622016 | tf_op jit(solution)/shard_map/all_gather | solution.py:38
  548.9 330.6 %all-gather.15.cloned.1.call-start = ((), (), s32[]{:S(2)}) async-start(), calls=%async_computation.4 | async-start | bytes 1622016 | tf_op jit(solution)/shard_map/all_gather | solution.py:32
  550.4 133.3 %collective-permute-start.1 = (f32[96,128]{1,0:T(8,128)}, f32[96,128]{1,0:T(8,128)}, u32[]{:S(2)}, u32[]{:S(2)}) collective-permute-start(f32[96,128]{1,0:T(8,128)} %get-tuple-element.5), channel_id=1, source_target_pairs={{32,0},{64,32},{96,64},{128,96},{160,128},{192,160},{224,192},{256... | collective-permute-start | bytes 147464 | tf_op jit(solution)/shard_map/ppermute | solution.py:17
  680.2 3.5 copy-start.5
  684.5 0.6 copy-start.3
  743.0 271.2 %all-gather.17.cloned.1.call-start = ((), (), s32[]{:S(2)}) async-start(), calls=%async_computation.5 | async-start | bytes 1622016 | tf_op jit(solution)/shard_map/all_gather | solution.py:38
  883.8 133.9 %collective-permute-start.2 = (f32[96,128]{1,0:T(8,128)S(1)}, f32[96,128]{1,0:T(8,128)S(1)}, u32[]{:S(2)}, u32[]{:S(2)}) collective-permute-start(f32[96,128]{1,0:T(8,128)S(1)} %get-tuple-element.3), channel_id=1, source_target_pairs={{32,0},{64,32},{96,64},{128,96},{160,128},{192,160},{224,192},{256... | collective-permute-start | bytes 147464 | tf_op jit(solution)/shard_map/ppermute | solution.py:17
Sparse Core Ops, SparseCore 0:
  66.5 144.3 all-gather.6
  214.8 131.2 all-gather.8
  409.1 136.2 all-gather.10
  549.0 131.1 all-gather.12
  743.2 136.2 all-gather.14
  883.0 131.1 all-gather.16
where the time goes:
time: 1030 us
  waiting for transfers between devices  803 us (78%)
  blocking collectives  171 us (17%)
  matrix products  21.1 us (2%)
  between operations  14.3 us (1%)
    all_gather x3, waiting for transfers between devices, body(): lax.all_gather(rhs, 'row', axis=0, tiled=True)  417 us
    all_gather x3, waiting for transfers between devices, body(): lax.all_gather(current, 'row', axis=0, tiled=True)  385 us
    psum x3, blocking collectives, broadcast(): return lax.psum(jnp.where(mine, array, jnp.zeros_like(array)), axis)  171 us
  transfers between devices with their start and end apart: 9, of which 6 were waited for; matrix products, arithmetic and copies ran while one was open for 1% of the time, Pallas kernels for 0%

commit v1 on v0

v1 whole, which is shorter than its diff:
```python
import functools

import jax
import jax.numpy as jnp
from jax import lax
from jax.experimental import pallas as pl
from jax.experimental.pallas import tpu as pltpu
from jax.sharding import PartitionSpec as P

MESH = pl.DeviceIdType.MESH
F32 = jnp.float32
BF16 = jnp.bfloat16
NG = 16
NP = 8
NZ = 16
RB = 96
U = 3072
PC = U // NP
HR = RB // 2


def split(x):
    hi = x.astype(BF16).astype(F32)
    return hi, x - hi


def kernel(
    lag_h, inv_h, hist_h, loads_h, cur_ref, fut_ref,
    lagv, invv, hist, loads, lb, wv, w0, w1, wl, xr, xf, tbuf, rbuf, inc, accs, pa,
    lsem, gs, gr, rss, rsr, lss, lsr, las, lar, lbs, lbr, pgs, pgr, sgs, sgr, shs, shr,
):
    g = lax.axis_index("lag")
    r = lax.axis_index("row")
    z, xl = r // 2, r % 2
    p, c = g // 2, g % 2
    xh = p % 2

    def rc(src, dst, ss, rs, gg, rr):
        return pltpu.make_async_remote_copy(
            src_ref=src, dst_ref=dst, send_sem=ss, recv_sem=rs, device_id=(gg, rr), device_id_type=MESH
        )

    def loop(n, f):
        lax.fori_loop(0, n, lambda i, _: (f(i), 0)[1], 0)

    barrier = pltpu.get_barrier_semaphore()

    def greet(gg, rr):
        pl.semaphore_signal(barrier, inc=1, device_id=(gg, rr), device_id_type=MESH)

    loop(2 * NZ - 1, lambda i: greet(g, (r + 1 + i) % (2 * NZ)))
    loop(NG - 1, lambda i: greet((g + 1 + i) % NG, r))
    loop(4, lambda i: greet(i * 4 + (1 - xh) * 2 + c, z * 2 + 1 - xl))

    loc = [
        pltpu.make_async_copy(inv_h, invv, lsem.at[0]),
        pltpu.make_async_copy(lag_h, lagv, lsem.at[1]),
        pltpu.make_async_copy(hist_h, hist, lsem.at[2]),
        pltpu.make_async_copy(loads_h, loads, lsem.at[3]),
    ]
    for cp in (loc[3], loc[2], loc[0], loc[1]):
        cp.start()
    root = pltpu.make_async_copy(lag_h, lb, lsem.at[4])

    @pl.when(g == 0)
    def _():
        root.start()

    loc[3].wait()
    loc[2].wait()

    def turned(n, h):
        d = loads[n] - hist[h]
        return jnp.concatenate([d, jnp.zeros((128 - RB, 128), F32)], axis=0).T.reshape(NG, 8, 128)

    @pl.when(g == 0)
    def _():
        t0 = turned(0, 0)
        tbuf[0] = t0
        rbuf[0] = t0[0]
        t1 = turned(1, 1)
        tbuf[1] = t1
        rbuf[1] = t1[0]
        root.wait()

    @pl.when(g == 1)
    def _():
        t2 = turned(2, 0)
        tbuf[2] = t2
        rbuf[2] = t2[1]

    pl.semaphore_wait(barrier, 2 * NZ - 1 + NG - 1 + 4)

    def rscatter(n, gg):
        return rc(tbuf.at[n, gg], rbuf.at[n], rss.at[n, gg], rsr.at[n], gg, r)

    def piece(n, cc, pp):
        return lb.at[n, pl.ds(pl.multiple_of(cc * HR, 8), HR), pl.ds(pl.multiple_of(pp * PC, 128), PC)]

    def lscatter(n, gg):
        v = piece(n, gg % 2, gg // 2)
        return rc(v, v, lss.at[n, gg], lsr.at[n], gg, r)

    @pl.when(g == 0)
    def _():
        loop(NG - 1, lambda i: rscatter(0, NG - 1 - i).start())
        loop(NG - 1, lambda i: lscatter(0, NG - 1 - i).start())
        loop(NG - 1, lambda i: rscatter(1, NG - 1 - i).start())
        loop(NG - 1, lambda i: lscatter(1, NG - 1 - i).start())

    @pl.when(g == 1)
    def _():
        loop(NG - 1, lambda i: rscatter(2, (g + 1 + i) % NG).start())

    def shift(n, src):
        return rc(src, inc.at[n], shs.at[n], shr.at[n], g - 1, r)

    @pl.when(g > 0)
    def _():
        shift(0, hist.at[0]).start()

    def prep(src, dst):
        dst[...] = jnp.zeros_like(dst)

        def some(i):
            blk = src[:, pl.ds(pl.multiple_of(i * 384, 128), 384)]
            for j in range(4):
                hi, lo = split(blk[:, j * RB : (j + 1) * RB])
                lanes = slice((j % 2) * 128, (j % 2) * 128 + RB)
                dst[2 * i + j // 2, 0:RB, lanes] = hi.astype(BF16)
                dst[2 * i + j // 2, 128 : 128 + RB, lanes] = lo.astype(BF16)

        loop(8, some)

    def prep_lags():
        wl[...] = jnp.zeros_like(wl)

        def some(i):
            for a in range(2):
                blk = lagv[a, :, pl.ds(pl.multiple_of(i * 384, 128), 384)]
                for j in range(4):
                    hi, lo = split(blk[:, j * RB : (j + 1) * RB])
                    wl[i, a * RB : (a + 1) * RB, j * 128 : j * 128 + RB] = hi.astype(BF16)
                    wl[i, (2 + a) * RB : (3 + a) * RB, j * 128 : j * 128 + RB] = lo.astype(BF16)

        loop(8, some)

    def at_turn(k):
        return (z + (2 * (k % 2) - 1) * (8 - (k + 1) // 2) + NZ) % NZ

    def block_to(xb, par, k, f):
        zz = at_turn(k)
        xx = (xl + 1 - f) % 2
        return rc(xb.at[z, xl], xb.at[z, xl], gs.at[par, 2 * k + f], gr.at[par, r], g, zz * 2 + xx)

    def block_from(xb, par, zz, xx):
        v = xb.at[zz, xx]
        return rc(v, v, gs.at[par, 0], gr.at[par, zz * 2 + xx], g, r)

    def send(xb, par, block):
        xb[z, xl] = block

        def one(i):
            block_to(xb, par, i // 2, i % 2).start()

        loop(2 * NZ - 1, one)

    def sent(xb, par):
        loop(2 * NZ - 1, lambda i: block_to(xb, par, i // 2, i % 2).wait_send())

    def product(xb, w, par=None):
        def one(i, acc):
            k = NZ - 1 - i
            zz = at_turn(k)
            if par is not None:
                block_from(xb, par, zz, 1 - xl).wait_recv()

                @pl.when(i > 0)
                def _():
                    block_from(xb, par, zz, xl).wait_recv()

            x = jnp.concatenate([xb[zz, 0], xb[zz, 1]], axis=1)
            hi, lo = split(x)
            lhs = jnp.concatenate([hi, lo], axis=0).astype(BF16)
            return acc + lax.dot_general(lhs, w[zz], (((1,), (1,)), ((), ())), preferred_element_type=F32)

        acc = lax.fori_loop(0, NZ, one, jnp.zeros((16, 256), F32))
        return (acc[0:8, 0:128] + acc[8:16, 0:128]) + (acc[0:8, 128:256] + acc[8:16, 128:256])

    def lgather(n, pp):
        v = piece(n, c, p)
        return rc(v, v, las.at[n, pp], lar.at[n, p], pp * 2 + c, r)

    def lgathered(n, pp):
        v = piece(n, c, pp)
        return rc(v, v, las.at[n, 0], lar.at[n, pp], g, r)

    def half(n, cc):
        return lb.at[n, pl.ds(pl.multiple_of(cc * HR, 8), HR), :]

    def lsib(n):
        return rc(half(n, c), half(n, c), lbs.at[n], lbr.at[n], g + 1 - 2 * c, r)

    def relay(n):
        @pl.when(g > 0)
        def _():
            lscatter(n, g).wait_recv()

        def one(i):
            pp = (p + 1 + i) % NP

            @pl.when(pp * 2 + c > 0)
            def _():
                lgather(n, pp).start()

        loop(NP - 1, one)

    def assemble(n):
        @pl.when(g > 0)
        def _():
            loop(NP - 1, lambda i: lgathered(n, (p + 1 + i) % NP).wait_recv())

        @pl.when(g != 1)
        def _():
            lsib(n).start()

        @pl.when(g > 0)
        def _():
            rc(half(n, 1 - c), half(n, 1 - c), lbs.at[n], lbr.at[n], g, r).wait_recv()

    def plane(n, pp):
        xx = (xl + (pp % 2 + xh) % 2) % 2
        return rc(xf.at[n, g], xf.at[n, g], pgs.at[n, pp], pgr.at[n, p], pp * 2 + c, z * 2 + xx)

    def planed(n, pp):
        v = xf.at[n, pp * 2 + c]
        return rc(v, v, pgs.at[n, 0], pgr.at[n, pp], g, r)

    def sib(n, pp):
        v = xf.at[n, pp * 2 + c]
        return rc(v, v, sgs.at[n, pp], sgr.at[n, pp], g + 1 - 2 * c, r)

    def sibbed(n, pp):
        v = xf.at[n, pp * 2 + 1 - c]
        return rc(v, v, sgs.at[n, 0], sgr.at[n, pp], g, r)

    def spread(n):
        sib(n, p).start()
        loop(NP - 1, lambda i: plane(n, (p + NP - 1 - i) % NP).start())

    def forward(n):
        def one(i):
            pp = (p + 1 + i) % NP
            planed(n, pp).wait_recv()
            sib(n, pp).start()

        loop(NP - 1, one)

    def lag_product(n):
        loop(NP, lambda i: sibbed(n, i).wait_recv())
        pa[...] = jnp.zeros_like(pa)

        def one(i):
            x = jnp.concatenate(
                [xf[n, :, 2 * i + j // 2, j % 2].reshape(128, 128) for j in range(4)], axis=1
            )
            hi, lo = split(x)
            rhs = jnp.concatenate([hi, lo], axis=0).astype(BF16)
            pa[...] += lax.dot_general(wl[i], rhs, (((1,), (1,)), ((), ())), preferred_element_type=F32)

        loop(8, one)

    def lag_rows(a):
        lo, hi = a * RB, (a + 1) * RB
        big = pa[lo:hi, 0:128] + pa[lo:hi, 128:256]
        small = pa[2 * RB + lo : 2 * RB + hi, 0:128] + pa[2 * RB + lo : 2 * RB + hi, 128:256]
        return big + small

    def incoming(n):
        @pl.when(g < NG - 1)
        def _():
            rc(inc.at[n], inc.at[n], shs.at[n], shr.at[n], g, r).wait_recv()

        @pl.when(g == NG - 1)
        def _():
            inc[n] = jnp.zeros((RB, 128), F32)

    def advance(n):
        lag_product(n)
        incoming(n)
        first = hist[1] if n == 0 else accs[n - 1, 1]
        accs[n, 0] = first + lag_rows(0)
        accs[n, 1] = inc[n] + lag_rows(1)

        @pl.when(g > 0)
        def _():
            shift(n + 1, accs.at[n, 0]).start()

    loc[0].wait()
    prep(invv, wv)
    loc[1].wait()

    def rwait(n):
        @pl.when(g != n // 2)
        def _():
            rscatter(n, g).wait_recv()

    rwait(0)
    send(xr.at[0], 0, rbuf[0])
    relay(0)
    prep_lags()
    now = product(xr.at[0], wv, 0)
    send(xf.at[0, g], 1, now)
    sent(xr.at[0], 0)
    relay(1)
    assemble(0)
    prep(lb.at[0], w0)
    rwait(1)
    now = rbuf[1] - product(xf.at[0, g], w0, 1)
    send(xr.at[1], 0, now)
    spread(0)
    sent(xf.at[0, g], 1)
    assemble(1)
    prep(lb.at[1], w1)
    rwait(2)
    late = rbuf[2] - product(xf.at[0, g], w1)
    now = product(xr.at[1], wv, 0)
    send(xf.at[1, g], 1, now)
    sent(xr.at[1], 0)
    forward(0)
    now = late - product(xf.at[1, g], w0, 1)
    send(xr.at[2], 0, now)
    spread(1)
    sent(xf.at[1, g], 1)
    advance(0)
    now = product(xr.at[2], wv, 0)
    send(xf.at[2, g], 1, now)
    sent(xr.at[2], 0)
    forward(1)
    advance(1)

    def arrived(i):
        zz = at_turn(NZ - 1 - i)
        block_from(xf.at[2, g], 1, zz, 1 - xl).wait_recv()

        @pl.when(i > 0)
        def _():
            block_from(xf.at[2, g], 1, zz, xl).wait_recv()

    loop(NZ, arrived)
    spread(2)
    sent(xf.at[2, g], 1)
    forward(2)
    lag_product(2)
    incoming(2)
    fut_ref[0] = accs[1, 1] + lag_rows(0)
    fut_ref[1] = inc[2] + lag_rows(1)
    cur_ref[...] = xf[2, :, z, xl].reshape(128, 128).T[0:RB]

    @pl.when(g == 0)
    def _():
        for n in range(2):
            loop(NG - 1, lambda i, n=n: rscatter(n, 1 + i).wait_send())
            loop(NG - 1, lambda i, n=n: lscatter(n, 1 + i).wait_send())

    @pl.when(g == 1)
    def _():
        loop(NG - 1, lambda i: rscatter(2, (g + 1 + i) % NG).wait_send())

    for n in range(2):

        def lsent(i, n=n):
            pp = (p + 1 + i) % NP

            @pl.when(pp * 2 + c > 0)
            def _():
                lgather(n, pp).wait_send()

        loop(NP - 1, lsent)

        @pl.when(g != 1)
        def _(n=n):
            lsib(n).wait_send()

    for n in range(3):
        loop(NP - 1, lambda i, n=n: plane(n, (p + 1 + i) % NP).wait_send())
        loop(NP, lambda i, n=n: sib(n, i).wait_send())

        @pl.when(g > 0)
        def _(n=n):
            shift(n, accs.at[0, 0]).wait_send()


def body(lag_ops, inverse, history, loads):
    anyspec = pl.BlockSpec(memory_space=pl.ANY)
    vspec = pl.BlockSpec(memory_space=pltpu.VMEM)
    dma = pltpu.SemaphoreType.DMA
    scratch = [
        pltpu.VMEM((2, RB, U), F32),
        pltpu.VMEM((RB, U), F32),
        pltpu.VMEM((2, RB, 128), F32),
        pltpu.VMEM((3, RB, 128), F32),
        pltpu.VMEM((2, RB, U), F32),
        pltpu.VMEM((NZ, 256, 256), BF16),
        pltpu.VMEM((NZ, 256, 256), BF16),
        pltpu.VMEM((NZ, 256, 256), BF16),
        pltpu.VMEM((8, 4 * RB, 512), BF16),
        pltpu.VMEM((3, NZ, 2, 8, 128), F32),
        pltpu.VMEM((3, NG, NZ, 2, 8, 128), F32),
        pltpu.VMEM((3, NG, 8, 128), F32),
        pltpu.VMEM((3, 8, 128), F32),
        pltpu.VMEM((3, RB, 128), F32),
        pltpu.VMEM((2, 2, RB, 128), F32),
        pltpu.VMEM((4 * RB, 256), F32),
        dma((5,)),
        dma((2, 2 * NZ)),
        dma((2, 2 * NZ)),
        dma((3, NG)),
        dma((3,)),
        dma((2, NG)),
        dma((2,)),
        dma((2, NP)),
        dma((2, NP)),
        dma((2,)),
        dma((2,)),
        dma((3, NP)),
        dma((3, NP)),
        dma((3, NP)),
        dma((3, NP)),
        dma((3,)),
        dma((3,)),
    ]
    return pl.pallas_call(
        kernel,
        out_shape=(
            jax.ShapeDtypeStruct((RB, 128), F32),
            jax.ShapeDtypeStruct((2, RB, 128), F32),
        ),
        in_specs=[anyspec] * 4,
        out_specs=(vspec, vspec),
        scratch_shapes=scratch,
        compiler_params=pltpu.CompilerParams(
            collective_id=0, has_side_effects=True, vmem_limit_bytes=48 * 2**20
        ),
    )(lag_ops, inverse, history, loads)


def solution(mesh):
    placed = (P("lag", "row", None), P("row", None), P("lag", "row", None), P(None, "row", None))
    return jax.shard_map(
        body,
        mesh=mesh,
        in_specs=placed,
        out_specs=(P("row", None), P("lag", "row", None)),
        check_vma=False,
    )
```

time: 1030 us -> 123 us (0.12)
  the two profiles are of different devices: /device:TPU:16 before, /device:TPU:1 now
where the time goes in v1:
time: 123 us
  Pallas kernels  116 us (94%)
  local copies, waits for them, and re-layouts  5.99 us (5%)
    pallas_call x1, Pallas kernels, body(): pl.pallas_call(kernel, out_shape=(jax.ShapeDtypeStruct((RB, 128), F32), j...  116 us
    unnamed x10, local copies, waits for them, and re-layouts  5.99 us

profile of v1, /device:TPU:1, one launch (start us, length us, event | category | flops | bytes accessed | tf_op | source)
XLA Modules:
  0.0 122.5 jit_solution(15103964774614855264)
XLA Ops:
  0.6 0.0 copy-start
  0.6 1.7 %copy-done = f32[2,96,3072]{2,1,0:T(8,128)S(1)} copy-done((f32[2,96,3072]{2,1,0:T(8,128)S(1)}, f32[2,96,3072]{2,1,0:T(8,128)}, u32[]{:S(2)}) %copy-start) | copy-done | bytes 2359320
  2.3 0.0 copy-start.1
  2.3 1.3 %copy-done.1 = f32[96,3072]{1,0:T(8,128)S(1)} copy-done((f32[96,3072]{1,0:T(8,128)S(1)}, f32[96,3072]{1,0:T(8,128)}, u32[]{:S(2)}) %copy-start.1) | copy-done | bytes 1179672
  3.6 0.0 copy-start.2
  3.6 0.9 copy-done.2
  4.5 0.0 copy-start.3
  4.5 0.9 copy-done.3
  5.4 115.9 %shard_map.59 = (f32[96,128]{1,0:T(8,128)S(1)}, f32[2,96,128]{2,1,0:T(8,128)S(1)}) custom-call(f32[2,96,3072]{2,1,0:T(8,128)S(1)} %copy-done, f32[96,3072]{1,0:T(8,128)S(1)} %copy-done.1, f32[2,96,128]{2,1,0:T(8,128)S(1)} %copy-done.3, f32[3,96,128]{2,1,0:T(8,128)S(1)} %copy-done.2), custom_call_target="tpu_custom_call" | custom-call | tf_op jit(solution)/shard_map/pallas_call | solution.py:433
  121.2 0.6 copy.8
  121.9 0.6 copy.9
Async XLA Ops:
  0.6 1.7 %copy-start = (f32[2,96,3072]{2,1,0:T(8,128)S(1)}, f32[2,96,3072]{2,1,0:T(8,128)}, u32[]{:S(2)}) copy-start(f32[2,96,3072]{2,1,0:T(8,128)} %lag_h.1) | copy-start | bytes 7077892
  2.3 1.3 %copy-start.1 = (f32[96,3072]{1,0:T(8,128)S(1)}, f32[96,3072]{1,0:T(8,128)}, u32[]{:S(2)}) copy-start(f32[96,3072]{1,0:T(8,128)} %inv_h.1) | copy-start | bytes 3538948
  3.6 0.9 copy-start.2
  4.5 0.9 copy-start.3

commit v2 on v1

v2 whole, which is shorter than its diff:
```python
import functools

import jax
import jax.numpy as jnp
from jax import lax
from jax.experimental import pallas as pl
from jax.experimental.pallas import tpu as pltpu
from jax.sharding import PartitionSpec as P

MESH = pl.DeviceIdType.MESH
F32 = jnp.float32
BF16 = jnp.bfloat16
NG = 16
NP = 8
NZ = 16
RB = 96
U = 3072
PC = U // NP
HR = RB // 2


def split(x):
    hi = x.astype(BF16).astype(F32)
    return hi, x - hi


def kernel(
    lag_h, inv_h, hist_h, loads_h, cur_ref, fut_ref,
    lagv, invv, hist, loads, lb, wv, w0, w1, wl, xr, xf, xc, tbuf, rbuf, inc, accs, pa,
    lsem, gs, gr, rss, rsr, lss, lsr, las, lar, lbs, lbr, pgs, pgr, sgs, sgr, shs, shr, qps, qpr, qss, qsr,
):
    g = lax.axis_index("lag")
    r = lax.axis_index("row")
    z, xl = r // 2, r % 2
    p, c = g // 2, g % 2
    xh = p % 2
    rx = (xl + xh) % 2

    def rc(src, dst, ss, rs, gg, rr):
        return pltpu.make_async_remote_copy(
            src_ref=src, dst_ref=dst, send_sem=ss, recv_sem=rs, device_id=(gg, rr), device_id_type=MESH
        )

    def loop(n, f):
        lax.fori_loop(0, n, lambda i, _: (f(i), 0)[1], 0)

    def over(pp):
        return z * 2 + (xl + xh + pp) % 2

    barrier = pltpu.get_barrier_semaphore()

    def greet(gg, rr):
        pl.semaphore_signal(barrier, inc=1, device_id=(gg, rr), device_id_type=MESH)

    loop(2 * NZ - 1, lambda i: greet(g, (r + 1 + i) % (2 * NZ)))
    loop(NG - 1, lambda i: greet((g + 1 + i) % NG, over((g + 1 + i) % NG // 2)))

    @pl.when((g > 0) & ((g - 1) // 2 % 2 != xh))
    def _():
        greet(g - 1, r)

    @pl.when((g < NG - 1) & ((g + 1) // 2 % 2 != xh))
    def _():
        greet(g + 1, r)

    extra = jnp.where((g > 0) & (g % 2 == 0), 1, 0) + jnp.where((g < NG - 1) & (g % 2 == 1), 1, 0)

    loc = [
        pltpu.make_async_copy(inv_h, invv, lsem.at[0]),
        pltpu.make_async_copy(lag_h, lagv, lsem.at[1]),
        pltpu.make_async_copy(hist_h, hist, lsem.at[2]),
        pltpu.make_async_copy(loads_h, loads, lsem.at[3]),
    ]
    for cp in (loc[3], loc[2], loc[0], loc[1]):
        cp.start()
    root = pltpu.make_async_copy(lag_h, lb, lsem.at[4])

    @pl.when(g == 0)
    def _():
        root.start()

    loc[3].wait()
    loc[2].wait()

    def turned(n, h):
        d = loads[n] - hist[h]
        return jnp.concatenate([d, jnp.zeros((128 - RB, 128), F32)], axis=0).T.reshape(NG, 8, 128)

    @pl.when(g == 0)
    def _():
        t0 = turned(0, 0)
        tbuf[0] = t0
        rbuf[0] = t0[0]
        t1 = turned(1, 1)
        tbuf[1] = t1
        rbuf[1] = t1[0]
        root.wait()

    @pl.when(g == 1)
    def _():
        t2 = turned(2, 0)
        tbuf[2] = t2
        rbuf[2] = t2[1]

    pl.semaphore_wait(barrier, 2 * NZ - 1 + NG - 1 + extra)

    def rscatter(n, gg):
        return rc(tbuf.at[n, gg], rbuf.at[n], rss.at[n, gg], rsr.at[n], gg, over(gg // 2))

    def piece(n, cc, pp):
        return lb.at[n, pl.ds(pl.multiple_of(cc * HR, 8), HR), pl.ds(pl.multiple_of(pp * PC, 128), PC)]

    def lscatter(n, gg):
        v = piece(n, gg % 2, gg // 2)
        return rc(v, v, lss.at[n, gg], lsr.at[n], gg, over(gg // 2))

    @pl.when(g == 0)
    def _():
        loop(NG - 1, lambda i: rscatter(0, NG - 1 - i).start())
        loop(NG - 1, lambda i: lscatter(0, NG - 1 - i).start())
        loop(NG - 1, lambda i: rscatter(1, NG - 1 - i).start())

    @pl.when(g == 1)
    def _():
        loop(NG - 1, lambda i: rscatter(2, (g + 1 + i) % NG).start())

    def shift(n, src):
        return rc(src, inc.at[n], shs.at[n], shr.at[n], g - 1, r)

    @pl.when(g > 0)
    def _():
        shift(0, hist.at[0]).start()

    def prep(src, dst):
        for f in range(2):
            dst[:, f * 128 + RB : (f + 1) * 128, :] = jnp.zeros((NZ, 128 - RB, 256), BF16)

        def some(i):
            blk = src[:, pl.ds(pl.multiple_of(i * 384, 128), 384)]
            hi, lo = split(jnp.concatenate([blk, jnp.zeros((128 - RB, 384), F32)], axis=0).T)
            hi, lo = hi.astype(BF16), lo.astype(BF16)
            for j in range(4):
                rows = slice((j % 2) * 128, (j % 2) * 128 + RB)
                dst[2 * i + j // 2, rows, 0:128] = hi[j * RB : (j + 1) * RB]
                dst[2 * i + j // 2, rows, 128:256] = lo[j * RB : (j + 1) * RB]

        loop(8, some)

    def prep_lags():
        def some(i):
            for a in range(2):
                blk = lagv[a, :, pl.ds(pl.multiple_of(i * 384, 128), 384)]
                for t in range(3):
                    tile = jnp.concatenate(
                        [blk[:, t * RB : (t + 1) * RB], blk[:, 288 + 32 * t : 320 + 32 * t]], axis=1
                    )
                    hi, lo = split(tile)
                    wl[i, a * RB : (a + 1) * RB, t * 128 : (t + 1) * 128] = hi.astype(BF16)
                    wl[i, (2 + a) * RB : (3 + a) * RB, t * 128 : (t + 1) * 128] = lo.astype(BF16)

        loop(8, some)

    def at_turn(k):
        return (z + (2 * (k % 2) - 1) * (8 - (k + 1) // 2) + NZ) % NZ

    def block_to(xb, par, k, f, own):
        zz = at_turn(k)
        xx = (xl + 1 - f) % 2
        v = xb.at[z, own]
        return rc(v, v, gs.at[par, 2 * k + f], gr.at[par, z * 2 + own], g, zz * 2 + xx)

    def block_from(xb, par, zz, xx):
        v = xb.at[zz, xx]
        return rc(v, v, gs.at[par, 0], gr.at[par, zz * 2 + xx], g, r)

    def send(xb, par, block, own):
        xb[z, own] = block

        def one(i):
            block_to(xb, par, i // 2, i % 2, own).start()

        loop(2 * NZ - 1, one)

    def sent(xb, par):
        loop(2 * NZ - 1, lambda i: block_to(xb, par, i // 2, i % 2, xl).wait_send())

    def arrived(xb, par, own, k):
        zz = at_turn(k)
        block_from(xb, par, zz, 1 - own).wait_recv()
        if k < NZ - 1:
            block_from(xb, par, zz, own).wait_recv()

    def product(xb, w, par=None, own=None):
        acc = [jnp.zeros((16, 256), F32), jnp.zeros((16, 256), F32)]
        for batch in ((15, 14, 13, 12, 11, 10, 9), (8, 7, 6, 5), (4, 3), (2, 1, 0)):
            if par is not None:
                for k in batch:
                    arrived(xb, par, own, k)
            for k in batch:
                zz = at_turn(k)
                x = jnp.concatenate([xb[zz, 0], xb[zz, 1]], axis=1)
                hi, lo = split(x)
                lhs = jnp.concatenate([hi, lo], axis=0).astype(BF16)
                acc[k % 2] += jnp.dot(lhs, w[zz], preferred_element_type=F32)
        acc = acc[0] + acc[1]
        return (acc[0:8, 0:128] + acc[8:16, 0:128]) + (acc[0:8, 128:256] + acc[8:16, 128:256])

    def lgather(n, pp):
        v = piece(n, c, p)
        return rc(v, v, las.at[n, pp], lar.at[n, p], pp * 2 + c, over(pp))

    def lgathered(n, pp):
        v = piece(n, c, pp)
        return rc(v, v, las.at[n, 0], lar.at[n, pp], g, r)

    def half(n, cc):
        return lb.at[n, pl.ds(pl.multiple_of(cc * HR, 8), HR), :]

    def lsib(n):
        return rc(half(n, c), half(n, c), lbs.at[n], lbr.at[n], g + 1 - 2 * c, r)

    def relay(n):
        @pl.when(g > 0)
        def _():
            lscatter(n, g).wait_recv()

        def one(i):
            pp = (p + 1 + i) % NP

            @pl.when(pp * 2 + c > 0)
            def _():
                lgather(n, pp).start()

        loop(NP - 1, one)

    def collect(n):
        @pl.when(g > 0)
        def _():
            loop(NP - 1, lambda i: lgathered(n, (p + 1 + i) % NP).wait_recv())

        @pl.when(g != 1)
        def _():
            lsib(n).start()

    def collected(n):
        @pl.when(g > 0)
        def _():
            rc(half(n, 1 - c), half(n, 1 - c), lbs.at[n], lbr.at[n], g, r).wait_recv()

    lane = lax.broadcasted_iota(jnp.int32, (8, 128), 1)

    def pack(n, i):
        last = xf[n, 2 * i + 1, 1]
        for t in range(3):
            xc[n, g, i, t] = jnp.where(
                lane < RB, xf[n, 2 * i + t // 2, t % 2], pltpu.roll(last, RB - 32 * t, 1)
            )

    def plane(n, pp):
        v = xc.at[n, g]
        return rc(v, v, pgs.at[n, pp], pgr.at[n, p], pp * 2 + c, over(pp))

    def planed(n, pp):
        v = xc.at[n, pp * 2 + c]
        return rc(v, v, pgs.at[n, 0], pgr.at[n, pp], g, r)

    def sib(n, pp):
        v = xc.at[n, pp * 2 + c]
        return rc(v, v, sgs.at[n, pp], sgr.at[n, pp], g + 1 - 2 * c, r)

    def sibbed(n, pp):
        v = xc.at[n, pp * 2 + 1 - c]
        return rc(v, v, sgs.at[n, 0], sgr.at[n, pp], g, r)

    def spread(n):
        loop(8, lambda i: pack(n, i))
        sib(n, p).start()
        loop(NP - 1, lambda i: plane(n, (p + NP - 1 - i) % NP).start())

    def forward(n):
        def one(i):
            pp = (p + 1 + i) % NP
            planed(n, pp).wait_recv()
            sib(n, pp).start()

        loop(NP - 1, one)

    def lag_part(n, i):
        x = jnp.concatenate([xc[n, :, i, t].reshape(128, 128) for t in range(3)], axis=1)
        hi, lo = split(x)
        rhs = jnp.concatenate([hi, lo], axis=0).astype(BF16)
        pa[...] += lax.dot_general(wl[i], rhs, (((1,), (1,)), ((), ())), preferred_element_type=F32)

    def lag_product(n):
        loop(NP, lambda i: sibbed(n, i).wait_recv())
        pa[...] = jnp.zeros_like(pa)
        loop(8, lambda i: lag_part(n, i))

    def turn(k):
        return (z // 2 + (1 - 2 * (k % 2)) * ((k + 1) // 2) + 8) % 8

    def qplane(i, pp):
        v = xc.at[2, g, i]
        return rc(v, v, qps.at[i, pp], qpr.at[i, p], pp * 2 + c, over(pp))

    def qplaned(i, pp):
        v = xc.at[2, pp * 2 + c, i]
        return rc(v, v, qps.at[i, 0], qpr.at[i, pp], g, r)

    def qsib(i, pp):
        v = xc.at[2, pp * 2 + c, i]
        return rc(v, v, qss.at[i, pp], qsr.at[i, pp], g + 1 - 2 * c, r)

    def qsibbed(i, pp):
        v = xc.at[2, pp * 2 + 1 - c, i]
        return rc(v, v, qss.at[i, 0], qsr.at[i, pp], g, r)

    def qspread(k):
        i = turn(k)
        pack(2, i)
        loop(NP - 1, lambda j: qplane(i, (p + NP - 1 - j) % NP).start())
        qsib(i, p).start()

    def qblock(zz, xx):
        @pl.when((zz != z) | (xx != xl))
        def _():
            block_from(xf.at[2], 1, zz, xx).wait_recv()

    def qgather(k):
        for j in range(4):
            qblock(2 * turn(k) + j // 2, j % 2)
        qspread(k)

    def qforward(k):
        i = turn(k)

        def one(j):
            pp = (p + 1 + j) % NP
            qplaned(i, pp).wait_recv()
            qsib(i, pp).start()

        loop(NP - 1, one)

    def qproduct(k):
        i = turn(k)
        loop(NP, lambda j: qsibbed(i, j).wait_recv())
        lag_part(2, i)

    def lag_rows(a):
        lo, hi = a * RB, (a + 1) * RB
        big = pa[lo:hi, 0:128] + pa[lo:hi, 128:256]
        small = pa[2 * RB + lo : 2 * RB + hi, 0:128] + pa[2 * RB + lo : 2 * RB + hi, 128:256]
        return big + small

    def incoming(n):
        @pl.when(g < NG - 1)
        def _():
            rc(inc.at[n], inc.at[n], shs.at[n], shr.at[n], g, r).wait_recv()

        @pl.when(g == NG - 1)
        def _():
            inc[n] = jnp.zeros((RB, 128), F32)

    def advance(n):
        lag_product(n)
        incoming(n)
        first = hist[1] if n == 0 else accs[n - 1, 1]
        accs[n, 0] = first + lag_rows(0)
        accs[n, 1] = inc[n] + lag_rows(1)

        @pl.when(g > 0)
        def _():
            shift(n + 1, accs.at[n, 0]).start()

    loc[0].wait()
    prep(invv, wv)
    loc[1].wait()

    def rwait(n):
        @pl.when(g != n // 2)
        def _():
            rscatter(n, g).wait_recv()

    rwait(0)
    send(xr.at[0], 0, rbuf[0], rx)
    relay(0)

    @pl.when(g == 0)
    def _():
        loop(NG - 1, lambda i: lscatter(1, NG - 1 - i).start())

    now = product(xr.at[0], wv, 0, rx)
    send(xf.at[0], 1, now, xl)
    sent(xr.at[0], 0)
    collect(0)
    relay(1)
    collected(0)
    prep(lb.at[0], w0)
    rwait(1)
    now = rbuf[1] - product(xf.at[0], w0, 1, xl)
    send(xr.at[1], 0, now, rx)
    spread(0)
    sent(xf.at[0], 1)
    prep_lags()
    collect(1)
    now = product(xr.at[1], wv, 0, rx)
    send(xf.at[1], 1, now, xl)
    sent(xr.at[1], 0)
    collected(1)
    prep(lb.at[1], w1)
    rwait(2)
    late = rbuf[2] - product(xf.at[0], w1)
    forward(0)
    now = late - product(xf.at[1], w0, 1, xl)
    send(xr.at[2], 0, now, rx)
    spread(1)
    sent(xf.at[1], 1)
    advance(0)
    now = product(xr.at[2], wv, 0, rx)
    send(xf.at[2], 1, now, xl)
    sent(xr.at[2], 0)
    loop(3, qgather)
    forward(1)
    loop(5, lambda k: qgather(k + 3))
    sent(xf.at[2], 1)
    advance(1)
    pa[...] = jnp.zeros_like(pa)
    qforward(0)

    def last(k):
        qforward(k + 1)
        qproduct(k)

    loop(7, last)
    m = z // 2
    own = 2 * (z % 2) + xl

    @pl.when(own < 3)
    def _():
        cur_ref[...] = xc[2, :, m, own].reshape(128, 128).T[0:RB]

    @pl.when(own == 3)
    def _():
        for t in range(3):
            cur_ref[32 * t : 32 * t + 32] = xc[2, :, m, t].reshape(128, 128).T[RB:128]

    incoming(2)
    qproduct(7)
    fut_ref[0] = accs[1, 1] + lag_rows(0)
    fut_ref[1] = inc[2] + lag_rows(1)

    @pl.when(g == 0)
    def _():
        for n in range(2):
            loop(NG - 1, lambda i, n=n: rscatter(n, 1 + i).wait_send())
            loop(NG - 1, lambda i, n=n: lscatter(n, 1 + i).wait_send())

    @pl.when(g == 1)
    def _():
        loop(NG - 1, lambda i: rscatter(2, (g + 1 + i) % NG).wait_send())

    for n in range(2):

        def lsent(i, n=n):
            pp = (p + 1 + i) % NP

            @pl.when(pp * 2 + c > 0)
            def _():
                lgather(n, pp).wait_send()

        loop(NP - 1, lsent)

        @pl.when(g != 1)
        def _(n=n):
            lsib(n).wait_send()

    def qsent(i):
        loop(NP - 1, lambda j: qplane(i, (p + 1 + j) % NP).wait_send())
        loop(NP, lambda j: qsib(i, j).wait_send())

    loop(8, qsent)
    for n in range(3):
        if n < 2:
            loop(NP - 1, lambda i, n=n: plane(n, (p + 1 + i) % NP).wait_send())
            loop(NP, lambda i, n=n: sib(n, i).wait_send())

        @pl.when(g > 0)
        def _(n=n):
            shift(n, accs.at[0, 0]).wait_send()


def body(lag_ops, inverse, history, loads):
    anyspec = pl.BlockSpec(memory_space=pl.ANY)
    vspec = pl.BlockSpec(memory_space=pltpu.VMEM)
    dma = pltpu.SemaphoreType.DMA
    scratch = [
        pltpu.VMEM((2, RB, U), F32),
        pltpu.VMEM((RB, U), F32),
        pltpu.VMEM((2, RB, 128), F32),
        pltpu.VMEM((3, RB, 128), F32),
        pltpu.VMEM((2, RB, U), F32),
        pltpu.VMEM((NZ, 256, 256), BF16),
        pltpu.VMEM((NZ, 256, 256), BF16),
        pltpu.VMEM((NZ, 256, 256), BF16),
        pltpu.VMEM((8, 4 * RB, 384), BF16),
        pltpu.VMEM((3, NZ, 2, 8, 128), F32),
        pltpu.VMEM((3, NZ, 2, 8, 128), F32),
        pltpu.VMEM((3, NG, 8, 3, 8, 128), F32),
        pltpu.VMEM((3, NG, 8, 128), F32),
        pltpu.VMEM((3, 8, 128), F32),
        pltpu.VMEM((3, RB, 128), F32),
        pltpu.VMEM((2, 2, RB, 128), F32),
        pltpu.VMEM((4 * RB, 256), F32),
        dma((5,)),
        dma((2, 2 * NZ)),
        dma((2, 2 * NZ)),
        dma((3, NG)),
        dma((3,)),
        dma((2, NG)),
        dma((2,)),
        dma((2, NP)),
        dma((2, NP)),
        dma((2,)),
        dma((2,)),
        dma((2, NP)),
        dma((2, NP)),
        dma((2, NP)),
        dma((2, NP)),
        dma((3,)),
        dma((3,)),
        dma((8, NP)),
        dma((8, NP)),
        dma((8, NP)),
        dma((8, NP)),
    ]
    return pl.pallas_call(
        kernel,
        out_shape=(
            jax.ShapeDtypeStruct((RB, 128), F32),
            jax.ShapeDtypeStruct((2, RB, 128), F32),
        ),
        in_specs=[anyspec] * 4,
        out_specs=(vspec, vspec),
        scratch_shapes=scratch,
        compiler_params=pltpu.CompilerParams(
            collective_id=0, has_side_effects=True, vmem_limit_bytes=60 * 2**20
        ),
    )(lag_ops, inverse, history, loads)


def solution(mesh):
    placed = (P("lag", "row", None), P("row", None), P("lag", "row", None), P(None, "row", None))
    return jax.shard_map(
        body,
        mesh=mesh,
        in_specs=placed,
        out_specs=(P("row", None), P("lag", "row", None)),
        check_vma=False,
    )
```

time: 123 us -> 100 us (0.81)
  Pallas kernels: 116 us -> 96.5 us
  local copies, waits for them, and re-layouts: 5.99 us -> 2.96 us
    pallas_call x1, Pallas kernels: 116 us -> 96.5 us  [body(): pl.pallas_call(kernel, out_shape=(jax.ShapeDtypeStruct((RB, 128), F32), j...]
    unnamed x10 -> x2, local copies, waits for them, and re-layouts: 5.99 us -> 2.96 us
where the time goes in v2:
time: 100 us
  Pallas kernels  96.5 us (96%)
  local copies, waits for them, and re-layouts  2.96 us (3%)
    pallas_call x1, Pallas kernels, body(): pl.pallas_call(kernel, out_shape=(jax.ShapeDtypeStruct((RB, 128), F32), j...  96.5 us
    unnamed x2, local copies, waits for them, and re-layouts  2.96 us

profile of v2, /device:TPU:1, one launch (start us, length us, event | category | flops | bytes accessed | tf_op | source)
XLA Modules:
  0.0 100.1 jit_solution(2209199538557278884)
XLA Ops:
  0.6 96.5 %shard_map.59 = (f32[96,128]{1,0:T(8,128)}, f32[2,96,128]{2,1,0:T(8,128)}) custom-call(f32[2,96,3072]{2,1,0:T(8,128)} %lag_h.1, f32[96,3072]{1,0:T(8,128)} %inv_h.1, f32[2,96,128]{2,1,0:T(8,128)} %hist_h.1, f32[3,96,128]{2,1,0:T(8,128)} %loads_h.1), custom_call_target="tpu_custom_call" | custom-call | tf_op jit(solution)/shard_map/pallas_call | solution.py:536
  97.2 1.4 %copy.8 = f32[96,128]{1,0:T(8,128)} copy(f32[96,128]{1,0:T(8,128)} %get-tuple-element.4) | data formatting | bytes 98304
  98.6 1.5 %copy.9 = f32[2,96,128]{2,1,0:T(8,128)} copy(f32[2,96,128]{2,1,0:T(8,128)} %get-tuple-element.5) | data formatting | bytes 196608

commit v3 on v2

--- a/solution.py
+++ b/solution.py
@@ -117,7 +117,7 @@
     @pl.when(g == 0)
     def _():
         loop(NG - 1, lambda i: rscatter(0, NG - 1 - i).start())
-        loop(NG - 1, lambda i: lscatter(0, NG - 1 - i).start())
+        loop(NG - 2, lambda i: lscatter(0, NG - 1 - i).start())
         loop(NG - 1, lambda i: rscatter(1, NG - 1 - i).start())
 
     @pl.when(g == 1)
@@ -131,32 +131,29 @@
     def _():
         shift(0, hist.at[0]).start()
 
-    def prep(src, dst):
+    def prep_zero(dst):
         for f in range(2):
             dst[:, f * 128 + RB : (f + 1) * 128, :] = jnp.zeros((NZ, 128 - RB, 256), BF16)
 
-        def some(i):
-            blk = src[:, pl.ds(pl.multiple_of(i * 384, 128), 384)]
-            hi, lo = split(jnp.concatenate([blk, jnp.zeros((128 - RB, 384), F32)], axis=0).T)
-            hi, lo = hi.astype(BF16), lo.astype(BF16)
-            for j in range(4):
-                rows = slice((j % 2) * 128, (j % 2) * 128 + RB)
-                dst[2 * i + j // 2, rows, 0:128] = hi[j * RB : (j + 1) * RB]
-                dst[2 * i + j // 2, rows, 128:256] = lo[j * RB : (j + 1) * RB]
-
-        loop(8, some)
+    def turned_parts(blk):
+        hi, lo = split(jnp.concatenate([blk, jnp.zeros((128 - RB, 384), F32)], axis=0).T)
+        return hi.astype(BF16), lo.astype(BF16)
+
+    def prep(src, dst, i):
+        hi, lo = turned_parts(src[:, pl.ds(pl.multiple_of(i * 384, 128), 384)])
+        for j in range(4):
+            rows = slice((j % 2) * 128, (j % 2) * 128 + RB)
+            dst[2 * i + j // 2, rows, 0:128] = hi[j * RB : (j + 1) * RB]
+            dst[2 * i + j // 2, rows, 128:256] = lo[j * RB : (j + 1) * RB]
 
     def prep_lags():
         def some(i):
             for a in range(2):
-                blk = lagv[a, :, pl.ds(pl.multiple_of(i * 384, 128), 384)]
-                for t in range(3):
-                    tile = jnp.concatenate(
-                        [blk[:, t * RB : (t + 1) * RB], blk[:, 288 + 32 * t : 320 + 32 * t]], axis=1
-                    )
-                    hi, lo = split(tile)
-                    wl[i, a * RB : (a + 1) * RB, t * 128 : (t + 1) * 128] = hi.astype(BF16)
-                    wl[i, (2 + a) * RB : (3 + a) * RB, t * 128 : (t + 1) * 128] = lo.astype(BF16)
+                hi, lo = turned_parts(lagv[a, :, pl.ds(pl.multiple_of(i * 384, 128), 384)])
+                for part, n in ((hi, a * 128), (lo, 256 + a * 128)):
+                    for t in range(3):
+                        wl[i, t * 128 : t * 128 + RB, n : n + 128] = part[t * RB : (t + 1) * RB]
+                        wl[i, t * 128 + RB : (t + 1) * 128, n : n + 128] = part[288 + 32 * t : 320 + 32 * t]
 
         loop(8, some)
 
@@ -180,6 +177,17 @@
             block_to(xb, par, i // 2, i % 2, own).start()
 
         loop(2 * NZ - 1, one)
+
+    def send_near(xb, par, block, own):
+        xb[z, own] = block
+        block_to(xb, par, 0, 0, own).start()
+        block_to(xb, par, 0, 1, own).start()
+
+        def one(i):
+            j = 2 * NZ - 2 - i
+            block_to(xb, par, j // 2, j % 2, own).start()
+
+        loop(2 * NZ - 3, one)
 
     def sent(xb, par):
         loop(2 * NZ - 1, lambda i: block_to(xb, par, i // 2, i % 2, xl).wait_send())
@@ -213,11 +221,13 @@
         v = piece(n, c, pp)
         return rc(v, v, las.at[n, 0], lar.at[n, pp], g, r)
 
-    def half(n, cc):
-        return lb.at[n, pl.ds(pl.multiple_of(cc * HR, 8), HR), :]
-
-    def lsib(n):
-        return rc(half(n, c), half(n, c), lbs.at[n], lbr.at[n], g + 1 - 2 * c, r)
+    def lsib(n, pp):
+        v = piece(n, c, pp)
+        return rc(v, v, lbs.at[n, pp], lbr.at[n, pp], g + 1 - 2 * c, r)
+
+    def lsibbed(n, pp):
+        v = piece(n, 1 - c, pp)
+        return rc(v, v, lbs.at[n, 0], lbr.at[n, pp], g, r)
 
     def relay(n):
         @pl.when(g > 0)
@@ -233,19 +243,35 @@
 
         loop(NP - 1, one)
 
+        @pl.when(g != 1)
+        def _():
+            lsib(n, p).start()
+
     def collect(n):
-        @pl.when(g > 0)
-        def _():
-            loop(NP - 1, lambda i: lgathered(n, (p + 1 + i) % NP).wait_recv())
-
-        @pl.when(g != 1)
-        def _():
-            lsib(n).start()
-
-    def collected(n):
-        @pl.when(g > 0)
-        def _():
-            rc(half(n, 1 - c), half(n, 1 - c), lbs.at[n], lbr.at[n], g, r).wait_recv()
+        def one(i):
+            pp = (p + 1 + i) % NP
+
+            @pl.when(g > 0)
+            def _():
+                lgathered(n, pp).wait_recv()
+
+            @pl.when(g != 1)
+            def _():
+                lsib(n, pp).start()
+
+        loop(NP - 1, one)
+
+    def prepare(n, dst):
+        def one(i):
+            pp = (p + i) % NP
+
+            @pl.when(g > 0)
+            def _():
+                lsibbed(n, pp).wait_recv()
+
+            prep(lb.at[n], dst, pp)
+
+        loop(NP, one)
 
     lane = lax.broadcasted_iota(jnp.int32, (8, 128), 1)
 
@@ -288,8 +314,9 @@
     def lag_part(n, i):
         x = jnp.concatenate([xc[n, :, i, t].reshape(128, 128) for t in range(3)], axis=1)
         hi, lo = split(x)
-        rhs = jnp.concatenate([hi, lo], axis=0).astype(BF16)
-        pa[...] += lax.dot_general(wl[i], rhs, (((1,), (1,)), ((), ())), preferred_element_type=F32)
+        lhs = jnp.concatenate([hi, lo], axis=0).astype(BF16)
+        o = jnp.dot(lhs, wl[i], preferred_element_type=F32)
+        pa[...] += (o[0:128, 0:256] + o[128:256, 0:256]) + (o[0:128, 256:512] + o[128:256, 256:512])
 
     def lag_product(n):
         loop(NP, lambda i: sibbed(n, i).wait_recv())
@@ -347,10 +374,7 @@
         lag_part(2, i)
 
     def lag_rows(a):
-        lo, hi = a * RB, (a + 1) * RB
-        big = pa[lo:hi, 0:128] + pa[lo:hi, 128:256]
-        small = pa[2 * RB + lo : 2 * RB + hi, 0:128] + pa[2 * RB + lo : 2 * RB + hi, 128:256]
-        return big + small
+        return pa[:, a * 128 : (a + 1) * 128].T[0:RB]
 
     def incoming(n):
         @pl.when(g < NG - 1)
@@ -372,8 +396,11 @@
         def _():
             shift(n + 1, accs.at[n, 0]).start()
 
+    prep_zero(wv)
     loc[0].wait()
-    prep(invv, wv)
+    loop(8, lambda i: prep(invv, wv, i))
+    for w in (w0, w1):
+        prep_zero(w)
     loc[1].wait()
 
     def rwait(n):
@@ -383,41 +410,45 @@
 
     rwait(0)
     send(xr.at[0], 0, rbuf[0], rx)
+
+    @pl.when(g == 0)
+    def _():
+        loop(NG - 2, lambda i: lscatter(0, NG - 1 - i).wait_send())
+        lscatter(0, 1).start()
+
     relay(0)
-
-    @pl.when(g == 0)
-    def _():
-        loop(NG - 1, lambda i: lscatter(1, NG - 1 - i).start())
-
     now = product(xr.at[0], wv, 0, rx)
     send(xf.at[0], 1, now, xl)
     sent(xr.at[0], 0)
+
+    @pl.when(g == 0)
+    def _():
+        loop(NG - 1, lambda i: lscatter(1, NG - 1 - i).start())
+
     collect(0)
-    relay(1)
-    collected(0)
-    prep(lb.at[0], w0)
+    prepare(0, w0)
     rwait(1)
     now = rbuf[1] - product(xf.at[0], w0, 1, xl)
     send(xr.at[1], 0, now, rx)
-    spread(0)
+    relay(1)
     sent(xf.at[0], 1)
     prep_lags()
-    collect(1)
     now = product(xr.at[1], wv, 0, rx)
     send(xf.at[1], 1, now, xl)
+    spread(0)
     sent(xr.at[1], 0)
-    collected(1)
-    prep(lb.at[1], w1)
+    collect(1)
+    prepare(1, w1)
     rwait(2)
     late = rbuf[2] - product(xf.at[0], w1)
-    forward(0)
     now = late - product(xf.at[1], w0, 1, xl)
     send(xr.at[2], 0, now, rx)
     spread(1)
     sent(xf.at[1], 1)
+    forward(0)
     advance(0)
     now = product(xr.at[2], wv, 0, rx)
-    send(xf.at[2], 1, now, xl)
+    send_near(xf.at[2], 1, now, xl)
     sent(xr.at[2], 0)
     loop(3, qgather)
     forward(1)
@@ -453,7 +484,7 @@
     def _():
         for n in range(2):
             loop(NG - 1, lambda i, n=n: rscatter(n, 1 + i).wait_send())
-            loop(NG - 1, lambda i, n=n: lscatter(n, 1 + i).wait_send())
+            loop(NG - 1 if n else 1, lambda i, n=n: lscatter(n, 1 + i).wait_send())
 
     @pl.when(g == 1)
     def _():
@@ -472,7 +503,7 @@
 
         @pl.when(g != 1)
         def _(n=n):
-            lsib(n).wait_send()
+            loop(NP, lambda i: lsib(n, i).wait_send())
 
     def qsent(i):
         loop(NP - 1, lambda j: qplane(i, (p + 1 + j) % NP).wait_send())
@@ -502,7 +533,7 @@
         pltpu.VMEM((NZ, 256, 256), BF16),
         pltpu.VMEM((NZ, 256, 256), BF16),
         pltpu.VMEM((NZ, 256, 256), BF16),
-        pltpu.VMEM((8, 4 * RB, 384), BF16),
+        pltpu.VMEM((8, 384, 512), BF16),
         pltpu.VMEM((3, NZ, 2, 8, 128), F32),
         pltpu.VMEM((3, NZ, 2, 8, 128), F32),
         pltpu.VMEM((3, NG, 8, 3, 8, 128), F32),
@@ -510,7 +541,7 @@
         pltpu.VMEM((3, 8, 128), F32),
         pltpu.VMEM((3, RB, 128), F32),
         pltpu.VMEM((2, 2, RB, 128), F32),
-        pltpu.VMEM((4 * RB, 256), F32),
+        pltpu.VMEM((128, 256), F32),
         dma((5,)),
         dma((2, 2 * NZ)),
         dma((2, 2 * NZ)),
@@ -520,8 +551,8 @@
         dma((2,)),
         dma((2, NP)),
         dma((2, NP)),
-        dma((2,)),
-        dma((2,)),
+        dma((2, NP)),
+        dma((2, NP)),
         dma((2, NP)),
         dma((2, NP)),
         dma((2, NP)),
@@ -536,8 +567,8 @@
     return pl.pallas_call(
         kernel,
         out_shape=(
-            jax.ShapeDtypeStruct((RB, 128), F32),
-            jax.ShapeDtypeStruct((2, RB, 128), F32),
+            pltpu.VMEM((RB, 128), F32),
+            pltpu.VMEM((2, RB, 128), F32),
         ),
         in_specs=[anyspec] * 4,
         out_specs=(vspec, vspec),

time: 100 us -> 93.9 us (0.939)
  Pallas kernels: 96.5 us -> 91.9 us
  local copies, waits for them, and re-layouts: 2.96 us -> 1.26 us
    pallas_call x1, Pallas kernels: 96.5 us -> 91.9 us  [body(): pl.pallas_call(kernel, out_shape=(pltpu.VMEM((RB, 128), F32), pltpu.VMEM(...]
    unnamed x2, local copies, waits for them, and re-layouts: 2.96 us -> 1.26 us
where the time goes in v3:
time: 93.9 us; the launch traced here: 93.8 us
  Pallas kernels  91.9 us (98%)
  local copies, waits for them, and re-layouts  1.26 us (1%)
    pallas_call x1, Pallas kernels, body(): pl.pallas_call(kernel, out_shape=(pltpu.VMEM((RB, 128), F32), pltpu.VMEM(...  91.9 us

profile of v3, /device:TPU:1, one launch (start us, length us, event | category | flops | bytes accessed | tf_op | source)
XLA Modules:
  0.0 93.8 jit_solution(14436780017139001552)
XLA Ops:
  0.6 91.9 %shard_map.59 = (f32[96,128]{1,0:T(8,128)S(1)}, f32[2,96,128]{2,1,0:T(8,128)S(1)}) custom-call(f32[2,96,3072]{2,1,0:T(8,128)} %lag_h.1, f32[96,3072]{1,0:T(8,128)} %inv_h.1, f32[2,96,128]{2,1,0:T(8,128)} %hist_h.1, f32[3,96,128]{2,1,0:T(8,128)} %loads_h.1), custom_call_target="tpu_custom_call" | custom-call | tf_op jit(solution)/shard_map/pallas_call | solution.py:567
  92.5 0.6 copy.8
  93.1 0.6 copy.9

commit v4 on v3

--- a/solution.py
+++ b/solution.py
@@ -455,12 +455,52 @@
     loop(5, lambda k: qgather(k + 3))
     sent(xf.at[2], 1)
     advance(1)
+    @pl.when(g == 0)
+    def _():
+        for n in range(2):
+            loop(NG - 1, lambda i, n=n: rscatter(n, 1 + i).wait_send())
+            loop(NG - 1 if n else 1, lambda i, n=n: lscatter(n, 1 + i).wait_send())
+
+    @pl.when(g == 1)
+    def _():
+        loop(NG - 1, lambda i: rscatter(2, (g + 1 + i) % NG).wait_send())
+
+    for n in range(2):
+
+        def lsent(i, n=n):
+            pp = (p + 1 + i) % NP
+
+            @pl.when(pp * 2 + c > 0)
+            def _():
+                lgather(n, pp).wait_send()
+
+        loop(NP - 1, lsent)
+
+        @pl.when(g != 1)
+        def _(n=n):
+            loop(NP, lambda i: lsib(n, i).wait_send())
+
+        loop(NP - 1, lambda i, n=n: plane(n, (p + 1 + i) % NP).wait_send())
+        loop(NP, lambda i, n=n: sib(n, i).wait_send())
+
+        @pl.when(g > 0)
+        def _(n=n):
+            shift(n, accs.at[0, 0]).wait_send()
+
+    def qplanesent(k):
+        loop(NP - 1, lambda j: qplane(turn(k), (p + 1 + j) % NP).wait_send())
+
+    def qsibsent(k):
+        loop(NP, lambda j: qsib(turn(k), j).wait_send())
+
     pa[...] = jnp.zeros_like(pa)
     qforward(0)
 
     def last(k):
         qforward(k + 1)
         qproduct(k)
+        qplanesent(k)
+        qsibsent(k)
 
     loop(7, last)
     m = z // 2
@@ -480,44 +520,12 @@
     fut_ref[0] = accs[1, 1] + lag_rows(0)
     fut_ref[1] = inc[2] + lag_rows(1)
 
-    @pl.when(g == 0)
-    def _():
-        for n in range(2):
-            loop(NG - 1, lambda i, n=n: rscatter(n, 1 + i).wait_send())
-            loop(NG - 1 if n else 1, lambda i, n=n: lscatter(n, 1 + i).wait_send())
-
-    @pl.when(g == 1)
-    def _():
-        loop(NG - 1, lambda i: rscatter(2, (g + 1 + i) % NG).wait_send())
-
-    for n in range(2):
-
-        def lsent(i, n=n):
-            pp = (p + 1 + i) % NP
-
-            @pl.when(pp * 2 + c > 0)
-            def _():
-                lgather(n, pp).wait_send()
-
-        loop(NP - 1, lsent)
-
-        @pl.when(g != 1)
-        def _(n=n):
-            loop(NP, lambda i: lsib(n, i).wait_send())
-
-    def qsent(i):
-        loop(NP - 1, lambda j: qplane(i, (p + 1 + j) % NP).wait_send())
-        loop(NP, lambda j: qsib(i, j).wait_send())
-
-    loop(8, qsent)
-    for n in range(3):
-        if n < 2:
-            loop(NP - 1, lambda i, n=n: plane(n, (p + 1 + i) % NP).wait_send())
-            loop(NP, lambda i, n=n: sib(n, i).wait_send())
-
-        @pl.when(g > 0)
-        def _(n=n):
-            shift(n, accs.at[0, 0]).wait_send()
+    qsibsent(7)
+    qplanesent(7)
+
+    @pl.when(g > 0)
+    def _():
+        shift(2, accs.at[0, 0]).wait_send()
 
 
 def body(lag_ops, inverse, history, loads):

time: 93.9 us -> 92 us (0.980)
  Pallas kernels: 91.9 us -> 90 us
    pallas_call x1, Pallas kernels: 91.9 us -> 90 us  [body(): pl.pallas_call(kernel, out_shape=(pltpu.VMEM((RB, 128), F32), pltpu.VMEM(...]
where the time goes in v4:
time: 92 us; the launch traced here: 91.9 us
  Pallas kernels  90 us (98%)
  local copies, waits for them, and re-layouts  1.26 us (1%)
    pallas_call x1, Pallas kernels, body(): pl.pallas_call(kernel, out_shape=(pltpu.VMEM((RB, 128), F32), pltpu.VMEM(...  90 us

profile of v4, /device:TPU:1, one launch (start us, length us, event | category | flops | bytes accessed | tf_op | source)
XLA Modules:
  0.0 91.9 jit_solution(8454218670798767496)
XLA Ops:
  0.6 90.0 %shard_map.59 = (f32[96,128]{1,0:T(8,128)S(1)}, f32[2,96,128]{2,1,0:T(8,128)S(1)}) custom-call(f32[2,96,3072]{2,1,0:T(8,128)} %lag_h.1, f32[96,3072]{1,0:T(8,128)} %inv_h.1, f32[2,96,128]{2,1,0:T(8,128)} %hist_h.1, f32[3,96,128]{2,1,0:T(8,128)} %loads_h.1), custom_call_target="tpu_custom_call" | custom-call | tf_op jit(solution)/shard_map/pallas_call | solution.py:575
  90.7 0.6 copy.8
  91.3 0.6 copy.9

commit v5 on v4

--- a/solution.py
+++ b/solution.py
@@ -282,6 +282,11 @@
                 lane < RB, xf[n, 2 * i + t // 2, t % 2], pltpu.roll(last, RB - 32 * t, 1)
             )
 
+    far_first = ((2, 1), (2, 0), (1, 1), (3, 1), (1, 0), (3, 0), (0, 1))
+
+    def peer(dy, dx):
+        return (p // 2 + dy) % 4 * 2 + (xh + dx) % 2
+
     def plane(n, pp):
         v = xc.at[n, g]
         return rc(v, v, pgs.at[n, pp], pgr.at[n, p], pp * 2 + c, over(pp))
@@ -301,7 +306,8 @@
     def spread(n):
         loop(8, lambda i: pack(n, i))
         sib(n, p).start()
-        loop(NP - 1, lambda i: plane(n, (p + NP - 1 - i) % NP).start())
+        for d in far_first:
+            plane(n, peer(*d)).start()
 
     def forward(n):
         def one(i):
@@ -345,7 +351,8 @@
     def qspread(k):
         i = turn(k)
         pack(2, i)
-        loop(NP - 1, lambda j: qplane(i, (p + NP - 1 - j) % NP).start())
+        for d in far_first:
+            qplane(i, peer(*d)).start()
         qsib(i, p).start()
 
     def qblock(zz, xx):
@@ -502,7 +509,7 @@
         qplanesent(k)
         qsibsent(k)
 
-    loop(7, last)
+    last(0)
     m = z // 2
     own = 2 * (z % 2) + xl
 
@@ -515,17 +522,19 @@
         for t in range(3):
             cur_ref[32 * t : 32 * t + 32] = xc[2, :, m, t].reshape(128, 128).T[RB:128]
 
+    loop(6, lambda k: last(k + 1))
     incoming(2)
+    qplanesent(7)
+
+    @pl.when(g > 0)
+    def _():
+        shift(2, accs.at[0, 0]).wait_send()
+
     qproduct(7)
     fut_ref[0] = accs[1, 1] + lag_rows(0)
     fut_ref[1] = inc[2] + lag_rows(1)
 
     qsibsent(7)
-    qplanesent(7)
-
-    @pl.when(g > 0)
-    def _():
-        shift(2, accs.at[0, 0]).wait_send()
 
 
 def body(lag_ops, inverse, history, loads):

time: 92 us -> 91.9 us (level)
  no operation moved by 1% of the time
where the time goes in v5:
time: 91.9 us; the launch traced here: 91.8 us
  Pallas kernels  89.9 us (98%)
  local copies, waits for them, and re-layouts  1.26 us (1%)
    pallas_call x1, Pallas kernels, body(): pl.pallas_call(kernel, out_shape=(pltpu.VMEM((RB, 128), F32), pltpu.VMEM(...  89.9 us

profile of v5, /device:TPU:1, one launch (start us, length us, event | category | flops | bytes accessed | tf_op | source)
XLA Modules:
  0.0 91.8 jit_solution(3652942332405144740)
XLA Ops:
  0.6 89.9 %shard_map.59 = (f32[96,128]{1,0:T(8,128)S(1)}, f32[2,96,128]{2,1,0:T(8,128)S(1)}) custom-call(f32[2,96,3072]{2,1,0:T(8,128)} %lag_h.1, f32[96,3072]{1,0:T(8,128)} %inv_h.1, f32[2,96,128]{2,1,0:T(8,128)} %hist_h.1, f32[3,96,128]{2,1,0:T(8,128)} %loads_h.1), custom_call_target="tpu_custom_call" | custom-call | tf_op jit(solution)/shard_map/pallas_call | solution.py:584
  90.5 0.6 copy.8
  91.1 0.6 copy.9
